TPU v7x, 32 devices: a whole 2x2x4 slice. The times are simulated.
32 devices in a mesh: dp: 8 (over z, y), mp: 4 (over x, core).
Axes of the slice: x: 2, y: 2, z: 4, core: 2. Of those that a mesh axis runs over, the one named last changes fastest.
Arguments:
- tokens: bfloat16 [128, 8192], P('dp', 'mp'), may hold values from -6 to 6
- gate_weight: bfloat16 [8192, 21504], P('mp', 'dp'), may hold values from -0.0625 to 0.0625
- up_weight: bfloat16 [8192, 21504], P('mp', 'dp'), may hold values from -0.0625 to 0.0625
- down_weight: bfloat16 [21504, 8192], P('dp', 'mp'), may hold values from -0.0390625 to 0.0390625
Outputs:
- mixed_out: bfloat16 [128, 8192], P('dp', 'mp')
All inputs are finite; a program needn't handle non-finite values.
Results may differ from a plain program's by a relative error of at most 0.005.
Values may be sent and summed in bfloat16 or wider, within the bound.
A program may use at most 128 MiB of HBM per device.

v0:
```python
import jax
import jax.numpy as jnp
from jax import lax
from jax.sharding import PartitionSpec as P


def swiglu(sums):
    return (jax.nn.silu(sums[:, 0, :]) * sums[:, 1, :]).astype(jnp.bfloat16)


def shards(tokens, gate_weight, up_weight, down_weight):
    paired = jnp.stack((gate_weight, up_weight), axis=1)
    partial_sums = jnp.einsum(
        "td,dkf->tkf",
        lax.all_gather(tokens, "dp", axis=0, tiled=True),
        paired,
        preferred_element_type=jnp.float32,
    )
    totals = lax.psum(partial_sums, "mp")
    hidden = swiglu(totals)
    mixed_out = lax.psum_scatter(
        jnp.dot(hidden, down_weight, preferred_element_type=jnp.float32),
        "dp",
        scatter_dimension=0,
        tiled=True,
    )
    return mixed_out.astype(jnp.bfloat16)


def solution(mesh):
    return jax.shard_map(
        shards,
        mesh=mesh,
        in_specs=(P("dp", "mp"), P("mp", "dp"), P("mp", "dp"), P("dp", "mp")),
        out_specs=P("dp", "mp"),
        check_vma=False,
    )
```

profile of v0, /device:TPU:0, one launch (start us, length us, event | category | flops | bytes accessed | tf_op | source)
XLA Modules:
  0.0 223.8 jit_solution(7592698520532821649)
XLA Ops:
  6.5 0.0 all-reduce.2.cloned.1.call-start
  6.5 33.2 %all_gather.3 = bf16[128,2048]{1,0:T(8,128)(2,1)S(1)} all-gather(bf16[16,2048]{1,0:T(8,128)(2,1)} %param.4), channel_id=1, replica_groups=mesh['dp'=8,'mp'=4] {'dp'}, dimensions={0}, use_global_device_ids=true | all-gather | bytes 589824 | tf_op jit(solution)/shard_map/all_gather | solution.py:15
  39.7 14.7 %copy.5 = bf16[2048,2688]{0,1:T(8,128)(2,1)} copy(bf16[2048,2688]{1,0:T(8,128)(2,1)} %param.5) | data formatting | bytes 22020096 | tf_op args[1]
  54.5 14.7 %copy.6 = bf16[2048,2688]{0,1:T(8,128)(2,1)} copy(bf16[2048,2688]{1,0:T(8,128)(2,1)} %param.6) | data formatting | bytes 22020096 | tf_op args[2]
  69.2 11.4 %fusion.4 = f32[128,2,2688]{0,2,1:T(8,128)} fusion(bf16[2048,1,2688]{0,2,1:T(8,128)(2,1)} %bitcast.21, bf16[2048,1,2688]{0,2,1:T(8,128)(2,1)} %bitcast.20, bf16[128,2048]{1,0:T(8,128)(2,1)S(1)} %all_gather.3), kind=kOutput, calls=%fused_computation.4 | convolution fusion | flops 2829582336 | bytes 25296896 | tf_op jit(solution)/shard_map/td,dkf->tkf/dot_general | solution.py:13
  80.7 0.0 all-reduce.2.cloned.1.call-update
  80.7 0.0 reduce-scatter.2.cloned.1.call-start
  80.7 63.3 %all-reduce.2.cloned.1.call-done = f32[128,2,2688]{0,2,1:T(8,128)} async-done(((f32[128,2,2688]{0,2,1:T(8,128)}), f32[128,2,2688]{0,2,1:T(8,128)}) %all-reduce.2.cloned.1.call-update) | async-done | bytes 2752528 | tf_op jit(solution)/shard_map/psum | solution.py:19
  144.0 7.7 %fusion.9 = f32[128,2048]{1,0:T(8,128)} fusion(bf16[2688,2048]{1,0:T(8,128)(2,1)} %param.7, f32[128,2,2688]{0,2,1:T(8,128)} %all-reduce.2.cloned.1.call-done), kind=kOutput, calls=%fused_computation.9 | convolution fusion | flops 1411350528 | bytes 14811136 | tf_op jit(solution)/shard_map/dot_general | solution.py:22
  151.7 0.0 reduce-scatter.2.cloned.1.call-update
  151.7 63.8 %reduce-scatter.2.cloned.1.call-done = f32[16,2048]{1,0:T(8,128)} async-done(((f32[128,2048]{1,0:T(8,128)}), f32[16,2048]{1,0:T(8,128)}) %reduce-scatter.2.cloned.1.call-update) | async-done | bytes 131088 | tf_op jit(solution)/shard_map/reduce_scatter | solution.py:21
  215.4 1.5 convert_element_type.7
Async XLA Ops:
  6.5 137.5 %all-reduce.2.cloned.1.call-start = ((), (), s32[]{:S(2)}) async-start(), calls=%async_computation.1 | async-start | bytes 5505024 | tf_op jit(solution)/shard_map/psum | solution.py:19
  80.7 134.8 %reduce-scatter.2.cloned.1.call-start = ((), (), s32[]{:S(2)}) async-start(), calls=%async_computation.2 | async-start | bytes 1179648 | tf_op jit(solution)/shard_map/reduce_scatter | solution.py:21
Sparse Core Ops, SparseCore 0:
  80.8 63.1 all-reduce.1
  151.8 63.5 reduce-scatter.1
where the time goes:
time: 225 us; the launch traced here: 224 us
  waiting for transfers between devices  127 us (56%)
  blocking collectives  33.2 us (15%)
  local copies, waits for them, and re-layouts  29.5 us (13%)
  matrix products  19.1 us (8%)
  between operations  13.4 us (6%)
    reduce_scatter x1, waiting for transfers between devices, shards(): lax.psum_scatter(jnp.dot(hidden, down_weight, preferred_element_type=jnp....  63.8 us
    psum x1, waiting for transfers between devices, shards(): totals = lax.psum(partial_sums, 'mp')  63.3 us
    all_gather x1, blocking collectives, shards(): lax.all_gather(tokens, 'dp', axis=0, tiled=True)  33.2 us
    unnamed x2, local copies, waits for them, and re-layouts  29.5 us
    dot_general x1, matrix products, shards(): jnp.einsum('td,dkf->tkf', lax.all_gather(tokens, 'dp', axis=0, tiled=True...  11.4 us
    dot_general x1, matrix products, shards(): jnp.dot(hidden, down_weight, preferred_element_type=jnp.float32)  7.67 us
  transfers between devices with their start and end apart: 2, of which 2 were waited for; matrix products, arithmetic and copies ran while one was open for 0% of the time, Pallas kernels for 0%

commit v1 on v0

--- a/solution.py
+++ b/solution.py
@@ -16,7 +16,8 @@
         paired,
         preferred_element_type=jnp.float32,
     )
-    totals = lax.psum(partial_sums, "mp")
+    parts = lax.all_gather(partial_sums, "mp")
+    totals = jnp.sum(parts, axis=0)
     hidden = swiglu(totals)
     mixed_out = lax.psum_scatter(
         jnp.dot(hidden, down_weight, preferred_element_type=jnp.float32),

time: 225 us -> 278 us (1.24)
  other arithmetic: 1.54 us -> 29.2 us
  local copies, waits for them, and re-layouts: 29.5 us -> 42.8 us
  waiting for transfers between devices: 127 us -> 139 us
    all_gather x0 -> x1, waiting for transfers between devices: none -> 75.9 us  [shards(): parts = lax.all_gather(partial_sums, 'mp')]
    psum x1 -> x0, waiting for transfers between devices: 63.3 us -> none  [shards(): totals = lax.psum(partial_sums, 'mp')]
    reduce_sum x0 -> x1, other arithmetic: none -> 27.6 us  [shards(): totals = jnp.sum(parts, axis=0)]
    all_gather x0 -> x1, local copies, waits for them, and re-layouts: none -> 13.4 us  [shards(): parts = lax.all_gather(partial_sums, 'mp')]
where the time goes in v1:
time: 278 us; the launch traced here: 276 us
  waiting for transfers between devices  139 us (50%)
  local copies, waits for them, and re-layouts  42.8 us (15%)
  blocking collectives  33.2 us (12%)
  other arithmetic  29.2 us (11%)
  matrix products  18.3 us (7%)
  between operations  13.4 us (5%)
    all_gather x1, waiting for transfers between devices, shards(): parts = lax.all_gather(partial_sums, 'mp')  75.9 us
    reduce_scatter x1, waiting for transfers between devices, shards(): lax.psum_scatter(jnp.dot(hidden, down_weight, preferred_element_type=jnp....  63.6 us
    all_gather x1, blocking collectives, shards(): lax.all_gather(tokens, 'dp', axis=0, tiled=True)  33.2 us
    unnamed x2, local copies, waits for them, and re-layouts  29.5 us
    reduce_sum x1, other arithmetic, shards(): totals = jnp.sum(parts, axis=0)  27.6 us
    all_gather x1, local copies, waits for them, and re-layouts, shards(): parts = lax.all_gather(partial_sums, 'mp')  13.4 us
    dot_general x1, matrix products, shards(): jnp.einsum('td,dkf->tkf', lax.all_gather(tokens, 'dp', axis=0, tiled=True...  11.4 us
    dot_general x1, matrix products, shards(): jnp.dot(hidden, down_weight, preferred_element_type=jnp.float32)  6.84 us
  transfers between devices with their start and end apart: 2, of which 2 were waited for; matrix products, arithmetic and copies ran while one was open for 0% of the time, Pallas kernels for 0%

profile of v1, /device:TPU:0, one launch (start us, length us, event | category | flops | bytes accessed | tf_op | source)
XLA Modules:
  0.0 276.4 jit_solution(16996834181343395410)
XLA Ops:
  6.5 0.0 all-gather.3.cloned.1.call-start
  6.5 33.2 %all_gather.9 = bf16[128,2048]{1,0:T(8,128)(2,1)S(1)} all-gather(bf16[16,2048]{1,0:T(8,128)(2,1)} %param.4), channel_id=1, replica_groups=mesh['dp'=8,'mp'=4] {'dp'}, dimensions={0}, use_global_device_ids=true | all-gather | bytes 589824 | tf_op jit(solution)/shard_map/all_gather | solution.py:15
  39.7 14.7 %copy.8 = bf16[2048,2688]{0,1:T(8,128)(2,1)} copy(bf16[2048,2688]{1,0:T(8,128)(2,1)} %param.5) | data formatting | bytes 22020096 | tf_op args[1]
  54.5 14.7 %copy.9 = bf16[2048,2688]{0,1:T(8,128)(2,1)} copy(bf16[2048,2688]{1,0:T(8,128)(2,1)} %param.6) | data formatting | bytes 22020096 | tf_op args[2]
  69.2 11.4 %fusion.4 = f32[128,2,2688]{0,2,1:T(8,128)} fusion(bf16[2048,1,2688]{0,2,1:T(8,128)(2,1)} %bitcast.23, bf16[2048,1,2688]{0,2,1:T(8,128)(2,1)} %bitcast.22, bf16[128,2048]{1,0:T(8,128)(2,1)S(1)} %all_gather.9), kind=kOutput, calls=%fused_computation.4 | convolution fusion | flops 2829582336 | bytes 25296896 | tf_op jit(solution)/shard_map/td,dkf->tkf/dot_general | solution.py:13
  80.7 0.0 all-gather.3.cloned.1.call-update
  80.7 0.0 reduce-scatter.2.cloned.1.call-start
  80.7 75.9 %all-gather.3.cloned.1.call-done = f32[512,2,2688]{0,2,1:T(8,128)} async-done(((f32[128,2,2688]{0,2,1:T(8,128)}), f32[512,2,2688]{0,2,1:T(8,128)}) %all-gather.3.cloned.1.call-update) | async-done | bytes 11010064 | tf_op jit(solution)/shard_map/all_gather | solution.py:19
  156.6 13.4 %reshape = f32[4,128,2,2688]{1,0,3,2:T(4,128)} reshape(f32[512,2,2688]{0,2,1:T(8,128)} %all-gather.3.cloned.1.call-done) | data formatting | bytes 22020096 | tf_op jit(solution)/shard_map/all_gather | solution.py:19
  170.0 27.6 %reduce_sum.9 = f32[128,2,2688]{0,2,1:T(8,128)S(1)} reduce(f32[4,128,2,2688]{1,0,3,2:T(4,128)} %reshape, f32[]{:T(128)} %constant.1.clone.1), dimensions={0}, to_apply=%region_0.0 | reduce | flops 2064384 | bytes 13762564 | tf_op jit(solution)/shard_map/reduce_sum | solution.py:20
  197.6 6.8 %fusion.9 = f32[128,2048]{1,0:T(8,128)} fusion(bf16[2688,2048]{1,0:T(8,128)(2,1)} %param.7, f32[128,2,2688]{0,2,1:T(8,128)S(1)} %reduce_sum.9), kind=kOutput, calls=%fused_computation.9 | convolution fusion | flops 1411350528 | bytes 14811136 | tf_op jit(solution)/shard_map/dot_general | solution.py:23
  204.4 0.0 reduce-scatter.2.cloned.1.call-update
  204.4 63.6 %reduce-scatter.2.cloned.1.call-done = f32[16,2048]{1,0:T(8,128)} async-done(((f32[128,2048]{1,0:T(8,128)}), f32[16,2048]{1,0:T(8,128)}) %reduce-scatter.2.cloned.1.call-update) | async-done | bytes 131088 | tf_op jit(solution)/shard_map/reduce_scatter | solution.py:22
  268.0 1.5 convert_element_type.7
Async XLA Ops:
  6.5 150.1 %all-gather.3.cloned.1.call-start = ((), (), s32[]{:S(2)}) async-start(), calls=%async_computation.2 | async-start | bytes 13762560 | tf_op jit(solution)/shard_map/all_gather | solution.py:19
  80.7 187.3 %reduce-scatter.2.cloned.1.call-start = ((), (), s32[]{:S(2)}) async-start(), calls=%async_computation.1 | async-start | bytes 1179648 | tf_op jit(solution)/shard_map/reduce_scatter | solution.py:22
Sparse Core Ops, SparseCore 0:
  80.8 75.7 all-gather.2
  204.6 63.4 reduce-scatter.1
